TPU v7x, 32 devices: a whole 2x2x4 slice. The times are simulated.
32 devices in a mesh: trow: 4 (over x, core), tcol: 4 (over z), visit: 2 (over y).
Axes of the slice: x: 2, y: 2, z: 4, core: 2. Of those that a mesh axis runs over, the one named last changes fastest.
Arguments:
- template: float32 [2048, 2048], P(('trow', 'visit'), 'tcol'), may hold values from -6 to 6
- warped: float32 [384, 256, 256], P(('trow', 'tcol', 'visit')), may hold values from -6 to 6
- coeffs: float32 [384, 27, 3], P(('trow', 'tcol', 'visit')), may hold values from -2 to 2
- dest_tile: int32 [384, 1], P(('trow', 'tcol', 'visit')), may hold values from 0 to 15; in each aligned block of 12 rows (0 to 11, 12 to 23, ...) at most 2 rows name the same one
- position: int32 [384, 1], P(('trow', 'tcol', 'visit')), may hold values from 0 to 3
Outputs:
- difference: float32 [384, 256, 256], P(('trow', 'tcol', 'visit'))
Inputs may be any that keep to these rules, and one draw needn't show every extreme that they name: `dest_tile`: tile index = tract row times the number of tract columns plus tract column; among the 12 blocks of one device no tile is named more than 2 times. `position`: sub-block row times 512 / 256 plus sub-block column.
All inputs are finite; a program needn't handle non-finite values.
Results may differ from a plain program's by a relative error of at most 0.0003.
Values sent between devices are 32-bit elements; how exact they have to be, the bound alone decides.
A program may use at most 192 MiB of HBM per device.

v0:
```python
import jax
import jax.numpy as jnp
import numpy as np
from jax import lax
from jax.experimental import pallas as pl
from jax.experimental.pallas import tpu as pltpu
from jax.sharding import PartitionSpec as P

BLK = 256
HALF = 10
SPREADS = (1.0, 2.0, 4.0)
DEGREES = (4, 2, 2)
STRIP = 128
EDGE = 16
SPAN = STRIP + 2 * EDGE
LANE = 128
FILTERS = [(s, k) for s in range(3) for k in range(DEGREES[s] + 1)]
DEPTH = -(-len(FILTERS) * SPAN // 256) * 256
POWERS = max(DEGREES) + 1


def taps():
    offsets = np.arange(-HALF, HALF + 1).astype(np.float64)
    table = {}
    for s, spread in enumerate(SPREADS):
        for k in range(DEGREES[s] + 1):
            weights = offsets**k * np.exp(-offsets * offsets / (2.0 * spread * spread))
            table[s, k] = weights / np.sqrt(np.sum(weights * weights))
    return table


def split(values):
    high = values.astype(jnp.bfloat16)
    return high, (values - high.astype(jnp.float32)).astype(jnp.bfloat16)


def constants():
    table = taps()
    index = {}
    for s, degree in enumerate(DEGREES):
        for i in range(degree + 1):
            for j in range(degree + 1 - i):
                index[s, i, j] = len(index)
    columns = np.zeros((2 * STRIP, len(FILTERS) * STRIP), np.float32)
    rows = np.zeros((POWERS, STRIP, DEPTH), np.float32)
    spread_out = np.zeros((len(index), POWERS, DEPTH), np.float32)
    for f, (s, k) in enumerate(FILTERS):
        for y in range(STRIP):
            columns[y : y + 2 * HALF + 1, f * STRIP + y] = table[s, k]
        for i in range(DEGREES[s] + 1 - k):
            spread_out[index[s, i, k], i, f * SPAN : (f + 1) * SPAN] = 1.0
            for x in range(STRIP):
                start = f * SPAN + x + EDGE - HALF
                rows[i, x, start : start + 2 * HALF + 1] = table[s, i]
    return columns, rows, spread_out.reshape(len(index), -1)


def mixing_kernel(coef_ref, rows_ref, out_ref):
    def mixed(q, lo, hi):
        total = None
        for i in range(POWERS):
            used = [f for f, (s, k) in enumerate(FILTERS) if i + k <= DEGREES[s]]
            if not any(f * SPAN < hi and (f + 1) * SPAN > lo for f in used):
                continue
            term = coef_ref[0, q : q + 1, i * DEPTH + lo : i * DEPTH + hi] * rows_ref[i, :, lo:hi]
            total = term if total is None else total + term
        return total

    place = lax.broadcasted_iota(jnp.int32, (STRIP, 1), 0).astype(jnp.float32)
    middle = (BLK - 1) / 2.0
    for lo in range(0, DEPTH, 256):
        hi = lo + 256
        flat, across, down = mixed(0, lo, hi), mixed(1, lo, hi), mixed(2, lo, hi)
        parts = [flat + (place + (STRIP * t - middle)) / middle * down for t in range(2)] + [across]
        for p, part in enumerate(parts):
            high, low = split(part)
            out_ref[0, p, 0, :, lo:hi] = high
            out_ref[0, p, 1, :, lo:hi] = low


def mixing(expanded, rows):
    blocks = expanded.shape[0]
    return pl.pallas_call(
        mixing_kernel,
        grid=(blocks,),
        in_specs=[
            pl.BlockSpec((1, 3, POWERS * DEPTH), lambda n: (n, 0, 0)),
            pl.BlockSpec((POWERS, STRIP, DEPTH), lambda n: (0, 0, 0)),
        ],
        out_specs=pl.BlockSpec((1, 3, 2, STRIP, DEPTH), lambda n: (n, 0, 0, 0, 0)),
        out_shape=jax.ShapeDtypeStruct((blocks, 3, 2, STRIP, DEPTH), jnp.bfloat16),
        compiler_params=pltpu.CompilerParams(vmem_limit_bytes=40 << 20),
        cost_estimate=pl.CostEstimate(
            flops=blocks * 40 * STRIP * DEPTH, bytes_accessed=blocks * 14 * STRIP * DEPTH, transcendentals=0
        ),
        name="row_matrices",
    )(expanded, rows)


def model_kernel(row_tiles, col_tiles, subs, tile_ref, place_ref, mix_ref, warped_ref, chigh_ref, clow_ref,
                 sky_ref, out_ref, window, bhigh, blow, sems):
    step = pl.program_id(0)
    steps = pl.num_programs(0)
    tile_rows = subs * BLK

    def corner(n):
        tile, place = tile_ref[n], place_ref[n]
        return (tile // col_tiles) * subs + place // subs, (tile % col_tiles) * subs + place % subs

    def copies(n, slot):
        a, b = corner(n)
        found = []
        for dr, (from_row, to_row, height) in enumerate(((BLK - EDGE, 0, EDGE), (0, EDGE, BLK), (0, EDGE + BLK, EDGE))):
            for dc, (from_col, to_col, width) in enumerate(((BLK - LANE, 0, LANE), (0, LANE, BLK), (0, LANE + BLK, LANE))):
                ra = jnp.clip(a + dr - 1, 0, row_tiles * subs - 1)
                cb = jnp.clip(b + dc - 1, 0, col_tiles * subs - 1)
                row = ((ra // subs) * col_tiles + cb // subs) * tile_rows + (ra % subs) * BLK + from_row
                col = (cb % subs) * BLK + from_col
                found.append(
                    pltpu.make_async_copy(
                        sky_ref.at[pl.ds(pl.multiple_of(row, EDGE), height), pl.ds(pl.multiple_of(col, LANE), width)],
                        window.at[slot, pl.ds(to_row, height), pl.ds(to_col, width)],
                        sems.at[slot, dr * 3 + dc],
                    )
                )
        return found

    @pl.when(step == 0)
    def _():
        used = len(FILTERS) * SPAN
        for t in range(2):
            bhigh[t, used:, :] = jnp.zeros((DEPTH - used, BLK), jnp.bfloat16)
            blow[t, used:, :] = jnp.zeros((DEPTH - used, BLK), jnp.bfloat16)
        for copy in copies(0, 0):
            copy.start()

    slot = lax.rem(step, 2)

    @pl.when(step + 1 < steps)
    def _():
        for copy in copies(step + 1, 1 - slot):
            copy.start()

    for copy in copies(step, slot):
        copy.wait()

    a, b = corner(step)
    rows_all, cols_all = BLK + 2 * EDGE, BLK + 2 * LANE

    @pl.when(a == 0)
    def _():
        window[slot, :EDGE, :] = jnp.zeros((EDGE, cols_all), jnp.float32)

    @pl.when(a == row_tiles * subs - 1)
    def _():
        window[slot, EDGE + BLK :, :] = jnp.zeros((EDGE, cols_all), jnp.float32)

    @pl.when(b == 0)
    def _():
        window[slot, :, :LANE] = jnp.zeros((rows_all, LANE), jnp.float32)

    @pl.when(b == col_tiles * subs - 1)
    def _():
        window[slot, :, LANE + BLK :] = jnp.zeros((rows_all, LANE), jnp.float32)

    dot = lambda x, y: jnp.dot(x, y, preferred_element_type=jnp.float32)
    shifted = pltpu.roll(window[slot], cols_all - (LANE - HALF), 1)
    high, low = split(shifted)
    high = jnp.concatenate([high[:, :BLK], high[:, STRIP : STRIP + BLK]], axis=0)
    low = jnp.concatenate([low[:, :BLK], low[:, STRIP : STRIP + BLK]], axis=0)
    for lo in range(0, len(FILTERS), 2):
        count = min(2, len(FILTERS) - lo)
        lanes = slice(lo * STRIP, (lo + count) * STRIP)
        chigh = chigh_ref[:, lanes]
        product = dot(high, chigh) + dot(low, chigh) + dot(high, clow_ref[:, lanes])
        phigh, plow = split(product)
        for f in range(count):
            for yt in range(2):
                for xt in range(2):
                    start = yt * rows_all + xt * STRIP
                    source = (slice(start, start + SPAN), slice(f * STRIP, (f + 1) * STRIP))
                    target = (xt, slice((lo + f) * SPAN, (lo + f + 1) * SPAN), slice(yt * STRIP, (yt + 1) * STRIP))
                    bhigh[target] = phigh[source]
                    blow[target] = plow[source]

    middle = (BLK - 1) / 2.0
    across = (lax.broadcasted_iota(jnp.int32, (1, BLK), 1).astype(jnp.float32) - middle) / middle
    for t in range(2):
        mhigh = jnp.concatenate([mix_ref[0, t, 0], mix_ref[0, 2, 0]], axis=0)
        mlow = jnp.concatenate([mix_ref[0, t, 1], mix_ref[0, 2, 1]], axis=0)
        right = bhigh[t]
        both = dot(mhigh, right) + dot(mlow, right) + dot(mhigh, blow[t])
        model = both[:STRIP] + across * both[STRIP:]
        rows = slice(t * STRIP, (t + 1) * STRIP)
        out_ref[0, rows, :] = warped_ref[0, rows, :] - model


def differences(sky, mix, warped, dest, place, row_tiles, col_tiles, subs, chigh, clow):
    blocks = warped.shape[0]
    rows_all, cols_all = BLK + 2 * EDGE, BLK + 2 * LANE

    def kernel(*refs):
        model_kernel(row_tiles, col_tiles, subs, *refs)

    return pl.pallas_call(
        kernel,
        grid_spec=pltpu.PrefetchScalarGridSpec(
            num_scalar_prefetch=2,
            grid=(blocks,),
            in_specs=[
                pl.BlockSpec((1, 3, 2, STRIP, DEPTH), lambda n, *_: (n, 0, 0, 0, 0)),
                pl.BlockSpec((1, BLK, BLK), lambda n, *_: (n, 0, 0)),
                pl.BlockSpec(chigh.shape, lambda n, *_: (0, 0)),
                pl.BlockSpec(clow.shape, lambda n, *_: (0, 0)),
                pl.BlockSpec(memory_space=pl.ANY),
            ],
            out_specs=pl.BlockSpec((1, BLK, BLK), lambda n, *_: (n, 0, 0)),
            scratch_shapes=[
                pltpu.VMEM((2, rows_all, cols_all), jnp.float32),
                pltpu.VMEM((2, DEPTH, BLK), jnp.bfloat16),
                pltpu.VMEM((2, DEPTH, BLK), jnp.bfloat16),
                pltpu.SemaphoreType.DMA((2, 9)),
            ],
        ),
        out_shape=jax.ShapeDtypeStruct(warped.shape, jnp.float32),
        compiler_params=pltpu.CompilerParams(vmem_limit_bytes=48 << 20),
        cost_estimate=pl.CostEstimate(
            flops=blocks * 2900000000, bytes_accessed=blocks * 4000000, transcendentals=0
        ),
        name="differences",
    )(dest, place, mix, warped, chigh, clow, sky)


def local_part(sky, warped, coeffs, dest, place, row_tiles, col_tiles, subs):
    columns, rows, spread_out = constants()
    chigh = columns.astype(jnp.bfloat16)
    clow = (columns - chigh.astype(np.float32)).astype(jnp.bfloat16)
    expanded = jnp.einsum("nbq,bk->nqk", coeffs, spread_out, precision=lax.Precision.HIGHEST)
    mix = mixing(expanded, jnp.asarray(rows))
    return differences(
        sky, mix, warped, dest, place, row_tiles, col_tiles, subs, jnp.asarray(chigh), jnp.asarray(clow)
    )


def gather_kernel(columns, order, own_ref, sky_ref, z_up, z_down, z_recv, f_send, f_recv, g_send, g_recv,
                  k_send, k_recv, local_sem):
    trow, tcol, visit = lax.axis_index("trow"), lax.axis_index("tcol"), lax.axis_index("visit")
    height = own_ref.shape[0]
    half = height // 2
    sibling = (trow + 1 - 2 * lax.rem(trow, 2), tcol, visit)
    across_x = (lax.rem(trow + 2, 4), tcol, visit)
    across_y = (trow, tcol, 1 - visit)
    above = (trow, tcol + 1, visit)
    below = (trow, tcol - 1, visit)
    has_above, has_below = tcol < columns - 1, tcol > 0

    barrier = pltpu.get_barrier_semaphore()

    def greet(device):
        pl.semaphore_signal(barrier, inc=1, device_id=device, device_id_type=pl.DeviceIdType.MESH)

    for device in (sibling, across_x, across_y):
        greet(device)

    @pl.when(has_above)
    def _():
        greet(above)

    @pl.when(has_below)
    def _():
        greet(below)

    pl.semaphore_wait(barrier, 3 + jnp.where(has_above, 1, 0) + jnp.where(has_below, 1, 0))

    def place(row, col, vis, h):
        start = ((row * columns + col) * 2 + vis) * height + h * half
        return sky_ref.at[pl.ds(pl.multiple_of(start, half), half), :]

    def remote(source, target, send, recv, device):
        return pltpu.make_async_remote_copy(
            src_ref=source, dst_ref=target, send_sem=send, recv_sem=recv,
            device_id=device, device_id_type=pl.DeviceIdType.MESH,
        )

    def home(h, w):
        swap_x = (w % 2 == 1) if h == 0 else (w >= 2)
        swap_y = (w >= 2) if h == 0 else (w % 2 == 1)
        return (lax.rem(trow + 2, 4) if swap_x else trow), (1 - visit if swap_y else visit)

    first = (across_x, across_y)
    second = (across_y, across_x)

    def slot(h, w, s):
        row, vis = home(h, w)
        return place(row, s, vis, h)

    def held(h, w, s, fresh):
        return own_ref.at[pl.ds(h * half, half), :] if fresh else slot(h, w, s)

    def up(h, s, fresh=False):
        return remote(held(h, 0, s, fresh), slot(h, 0, s), z_up.at[h, s], z_recv.at[h, s], above)

    def down(h, s, fresh=False):
        return remote(held(h, 0, s, fresh), slot(h, 0, s), z_down.at[h, s], z_recv.at[h, s], below)

    def one(h, s, fresh=False):
        return remote(held(h, 0, s, fresh), slot(h, 0, s), f_send.at[h, s], f_recv.at[h, s], first[h])

    def two(h, w, s, fresh=False):
        return remote(held(h, w, s, fresh), slot(h, w, s), g_send.at[h, w, s], g_recv.at[h, w, s], second[h])

    def hand(h, w, s, fresh=False):
        return remote(held(h, w, s, fresh), slot(h, w, s), k_send.at[h, w, s], k_recv.at[h, w, s], sibling)

    spots = []
    for j in range(columns):
        s = jnp.int32(0)
        for z in range(columns):
            s = jnp.where(tcol == z, order[z][j], s)
        spots.append(s)

    mine = pltpu.make_async_copy(own_ref, sky_ref.at[
        pl.ds(pl.multiple_of(((trow * columns + tcol) * 2 + visit) * height, height), height), :], local_sem)
    mine.start()

    def moves_up(s):
        return jnp.logical_and(has_above, s <= tcol)

    def moves_down(s):
        return jnp.logical_and(has_below, s >= tcol)

    def column_item(h, s, fresh):
        @pl.when(moves_up(s))
        def _():
            up(h, s, fresh).start()

        @pl.when(moves_down(s))
        def _():
            down(h, s, fresh).start()

        one(h, s, fresh).start()
        two(h, 0, s, fresh).start()
        hand(h, 0, s, fresh).start()

    def partner_item(h, s):
        one_in = remote(slot(h, 1, s), slot(h, 1, s), f_send.at[h, s], f_recv.at[h, s], first[h])
        one_in.wait_recv()
        two(h, 1, s).start()
        hand(h, 1, s).start()

    for j, s in enumerate(spots):
        for h in range(2):
            if j > 0:
                up_in = remote(slot(h, 0, s), slot(h, 0, s), z_up.at[h, s], z_recv.at[h, s], across_x)
                up_in.wait_recv()
            column_item(h, s, j == 0)
        if j > 0:
            for h in range(2):
                partner_item(h, spots[j - 1])
    for h in range(2):
        partner_item(h, spots[-1])
    for w in range(2):
        for s in spots:
            for h in range(2):
                two_in = remote(
                    slot(h, 2 + w, s), slot(h, 2 + w, s), g_send.at[h, w, s], g_recv.at[h, w, s], second[h]
                )
                two_in.wait_recv()
                hand(h, 2 + w, s).start()

    other = lax.rem(trow, 2)
    for j, s in enumerate(spots):
        for h in range(2):
            for w in range(4):
                row, vis = home(h, w)
                landed = place(row + 1 - 2 * other, s, vis, h)
                remote(landed, landed, k_send.at[h, w, s], k_recv.at[h, w, s], sibling).wait_recv()
    mine.wait()
    for j, s in enumerate(spots):
        fresh = j == 0
        for h in range(2):
            @pl.when(moves_up(s))
            def _():
                up(h, s, fresh).wait_send()

            @pl.when(moves_down(s))
            def _():
                down(h, s, fresh).wait_send()

            one(h, s, fresh).wait_send()
            for w in range(2):
                two(h, w, s, fresh and w == 0).wait_send()
            for w in range(4):
                hand(h, w, s, fresh and w == 0).wait_send()


def gathered(template, columns, devices):
    order = [sorted(range(columns), key=lambda s: (abs(s - z), s)) for z in range(columns)]
    dma = pltpu.SemaphoreType.DMA

    def kernel(*refs):
        gather_kernel(columns, order, *refs)

    return pl.pallas_call(
        kernel,
        in_specs=[pl.BlockSpec(memory_space=pl.ANY)],
        out_specs=pl.BlockSpec(memory_space=pl.ANY),
        out_shape=jax.ShapeDtypeStruct((devices * template.shape[0], template.shape[1]), template.dtype),
        scratch_shapes=[
            dma((2, columns)), dma((2, columns)), dma((2, columns)),
            dma((2, columns)), dma((2, columns)),
            dma((2, 2, columns)), dma((2, 2, columns)),
            dma((2, 4, columns)), dma((2, 4, columns)),
            dma,
        ],
        compiler_params=pltpu.CompilerParams(
            collective_id=0, has_side_effects=True, vmem_limit_bytes=60 << 20
        ),
        cost_estimate=pl.CostEstimate(
            flops=0, bytes_accessed=2 * devices * template.size * 4, transcendentals=0
        ),
        name="gather_template",
    )(template)


def on_device(template, warped, coeffs, dest_tile, position):
    axes = ("trow", "tcol", "visit")
    sizes = [lax.axis_size(axis) for axis in axes]
    if sizes[0] == 4 and sizes[2] == 2:
        sky = gathered(template, sizes[1], sizes[0] * sizes[1] * sizes[2])
    else:
        sky = lax.all_gather(template, axes, axis=0, tiled=True)
    subs = template.shape[1] // BLK
    return local_part(
        sky, warped, coeffs, dest_tile[:, 0], position[:, 0],
        lax.axis_size("trow"), lax.axis_size("tcol"), subs,
    )


def solution(mesh):
    return jax.shard_map(
        on_device,
        mesh=mesh,
        in_specs=(
            P(("trow", "visit"), "tcol"),
            P(("trow", "tcol", "visit"), None, None),
            P(("trow", "tcol", "visit"), None, None),
            P(("trow", "tcol", "visit"), None),
            P(("trow", "tcol", "visit"), None),
        ),
        out_specs=P(("trow", "tcol", "visit"), None, None),
        check_vma=False,
    )
```

profile of v0, /device:TPU:1, one launch (start us, length us, event | category | flops | bytes accessed | tf_op | source)
XLA Modules:
  0.0 142.8 jit_solution(7855608264575897631)
XLA Ops:
  0.0 0.0 copy-start
  0.0 0.7 copy-done
  0.7 2.7 %fusion = f32[8960,12,3]{0,1,2:T(8,128)S(1)} fusion(f32[27,8960,1]{1,0,2:T(8,128)} %constant.16, f32[12,27,3]{1,2,0:T(4,128)S(1)} %copy-done), kind=kOutput, calls=%fused_computation.1 | convolution fusion | flops 104509440 | bytes 2261808 | tf_op jit(solution)/shard_map/nbq,bk->nqk/dot_general | solution.py:238
  3.5 0.9 copy.15
  4.4 75.9 %gather_template.1.refs_6_ = f32[8192,512]{1,0:T(8,128)} custom-call(f32[256,512]{1,0:T(8,128)} %refs_0_.1), custom_call_target="tpu_custom_call" | custom-call | bytes 33554432 | tf_op jit(solution)/shard_map/gather_template/pallas_call | solution.py:404
  80.3 0.0 copy-start.2
  80.3 2.3 %copy-done.2 = f32[5,128,1792]{2,1,0:T(8,128)S(1)} copy-done((f32[5,128,1792]{2,1,0:T(8,128)S(1)}, f32[5,128,1792]{2,1,0:T(8,128)}, u32[]{:S(2)}) %copy-start.2) | copy-done | bytes 4587544
  82.6 0.0 copy-start.3
  82.6 0.0 copy-start.4
  82.6 0.0 copy-start.5
  82.6 0.0 copy-start.6
  82.7 0.0 copy-start.7
  82.7 15.9 %row_matrices.1.refs_2_ = bf16[12,3,2,128,1792]{4,3,2,1,0:T(8,128)(2,1)} custom-call(f32[12,3,8960]{2,1,0:T(4,128)S(1)} %bitcast.7, f32[5,128,1792]{2,1,0:T(8,128)S(1)} %copy-done.2), custom_call_target="tpu_custom_call" | custom-call | flops 110100480 | bytes 38535168 | tf_op jit(solution)/shard_map/row_matrices/pallas_call | solution.py:83
  98.6 0.0 copy-done.3
  98.6 0.0 copy-done.4
  98.6 0.0 copy-done.5
  98.6 0.0 copy-done.6
  98.6 0.0 copy-done.7
  98.6 0.0 copy-start.1
  98.6 44.1 %differences.1 = f32[12,256,256]{2,1,0:T(8,128)} custom-call(s32[12]{0:T(128)S(1)} %bitcast.8, s32[12]{0:T(128)S(1)} %bitcast.9, bf16[12,3,2,128,1792]{4,3,2,1,0:T(8,128)(2,1)} %row_matrices.1.refs_2_, f32[12,256,256]{2,1,0:T(8,128)S(1)} %copy-done.3, bf16[256,1408]{1,0:T(8,128)(2,1)S(1)} %copy-done.7, bf16[256,1408]{1,0:T(8,128)(2,1)S(1)} %copy-done.6, ...), custom_call_target="tpu_custom_call" | custom-call | flops 34800001024 | bytes 48000000 | tf_op jit(solution)/shard_map/differences/pallas_call | solution.py:205
  142.8 0.0 copy-done.1
Async XLA Ops:
  0.0 0.7 copy-start
  80.3 2.3 %copy-start.2 = (f32[5,128,1792]{2,1,0:T(8,128)S(1)}, f32[5,128,1792]{2,1,0:T(8,128)}, u32[]{:S(2)}) copy-start(f32[5,128,1792]{2,1,0:T(8,128)} %constant.9.clone.rows_ref) | copy-start | bytes 13762564
  82.6 16.0 %copy-start.3 = (f32[12,256,256]{2,1,0:T(8,128)S(1)}, f32[12,256,256]{2,1,0:T(8,128)}, u32[]{:S(2)}) copy-start(f32[12,256,256]{2,1,0:T(8,128)} %refs_3_.1) | copy-start | bytes 9437188
  82.6 16.0 %copy-start.4 = (s32[12,1]{0,1:T(1,128)S(1)}, s32[12,1]{0,1:T(1,128)}, u32[]{:S(2)}) copy-start(s32[12,1]{0,1:T(1,128)} %param.12) | copy-start | bytes 148
  82.6 16.0 %copy-start.5 = (s32[12,1]{0,1:T(1,128)S(1)}, s32[12,1]{0,1:T(1,128)}, u32[]{:S(2)}) copy-start(s32[12,1]{0,1:T(1,128)} %param.13) | copy-start | bytes 148
  82.6 16.0 %copy-start.6 = (bf16[256,1408]{1,0:T(8,128)(2,1)S(1)}, bf16[256,1408]{1,0:T(8,128)(2,1)}, u32[]{:S(2)}) copy-start(bf16[256,1408]{1,0:T(8,128)(2,1)} %constant.11.clone.refs_5_) | copy-start | bytes 2162692
  82.7 16.0 %copy-start.7 = (bf16[256,1408]{1,0:T(8,128)(2,1)S(1)}, bf16[256,1408]{1,0:T(8,128)(2,1)}, u32[]{:S(2)}) copy-start(bf16[256,1408]{1,0:T(8,128)(2,1)} %constant.10.clone.refs_4_) | copy-start | bytes 2162692
  98.6 44.2 %copy-start.1 = (f32[12,27,3]{1,2,0:T(4,128)S(1)}, f32[12,27,3]{1,2,0:T(4,128)}, u32[]{:S(2)}) copy-start(f32[12,27,3]{1,2,0:T(4,128)} %param.11) | copy-start | bytes 11668
where the time goes:
time: 143 us
  Pallas kernels  136 us (95%)
  local copies, waits for them, and re-layouts  3.95 us (3%)
  matrix products  2.75 us (2%)
    pallas_call x1, Pallas kernels, gathered(): pl.pallas_call(kernel, in_specs=[pl.BlockSpec(memory_space=pl.ANY)], out_...  75.9 us
    pallas_call x1, Pallas kernels, differences(): pl.pallas_call(kernel, grid_spec=pltpu.PrefetchScalarGridSpec(num_scalar_...  44.1 us
    pallas_call x1, Pallas kernels, mixing(): pl.pallas_call(mixing_kernel, grid=(blocks,), in_specs=[pl.BlockSpec((1,...  15.9 us
    unnamed x16, local copies, waits for them, and re-layouts  3.06 us

commit v1 on v0

--- a/solution.py
+++ b/solution.py
@@ -231,19 +231,18 @@
     )(dest, place, mix, warped, chigh, clow, sky)
 
 
-def local_part(sky, warped, coeffs, dest, place, row_tiles, col_tiles, subs):
-    columns, rows, spread_out = constants()
+def local_part(sky, mix, warped, dest, place, row_tiles, col_tiles, subs):
+    columns = constants()[0]
     chigh = columns.astype(jnp.bfloat16)
     clow = (columns - chigh.astype(np.float32)).astype(jnp.bfloat16)
-    expanded = jnp.einsum("nbq,bk->nqk", coeffs, spread_out, precision=lax.Precision.HIGHEST)
-    mix = mixing(expanded, jnp.asarray(rows))
     return differences(
         sky, mix, warped, dest, place, row_tiles, col_tiles, subs, jnp.asarray(chigh), jnp.asarray(clow)
     )
 
 
-def gather_kernel(columns, order, own_ref, sky_ref, z_up, z_down, z_recv, f_send, f_recv, g_send, g_recv,
-                  k_send, k_recv, local_sem):
+def gather_kernel(columns, order, own_ref, coef_ref, spread_ref, rows_ref, sky_ref, mix_ref, z_up, z_down, z_recv,
+                  f_send, f_recv, g_send, g_recv, k_send, k_recv, local_sem, coef, spread, rows, expanded, stage,
+                  load_sems, store_sems):
     trow, tcol, visit = lax.axis_index("trow"), lax.axis_index("tcol"), lax.axis_index("visit")
     height = own_ref.shape[0]
     half = height // 2
@@ -323,6 +322,53 @@
         pl.ds(pl.multiple_of(((trow * columns + tcol) * 2 + visit) * height, height), height), :], local_sem)
     mine.start()
 
+    loads = [
+        pltpu.make_async_copy(source, target, load_sems.at[k])
+        for k, (source, target) in enumerate(((coef_ref, coef), (spread_ref, spread), (rows_ref, rows)))
+    ]
+    for load in loads:
+        load.start()
+    blocks = mix_ref.shape[0]
+    stores = [pltpu.make_async_copy(stage.at[n % 2], mix_ref.at[n], store_sems.at[n % 2]) for n in range(blocks)]
+    middle = (BLK - 1) / 2.0
+
+    def build(n):
+        if n == 0:
+            for load in loads:
+                load.wait()
+            expanded[...] = jnp.dot(
+                coef[...], spread[...], precision=lax.Precision.HIGHEST, preferred_element_type=jnp.float32
+            )
+        if n >= 2:
+            stores[n - 2].wait()
+
+        def chunk(c, carry):
+            lo = pl.multiple_of(c * LANE, LANE)
+            flat, across, down = [
+                sum(
+                    expanded[3 * n + q : 3 * n + q + 1, pl.ds(pl.multiple_of(i * DEPTH + lo, LANE), LANE)]
+                    * rows[i, :, pl.ds(lo, LANE)]
+                    for i in range(POWERS)
+                )
+                for q in range(3)
+            ]
+            place_in = lax.broadcasted_iota(jnp.int32, (STRIP, 1), 0).astype(jnp.float32)
+            parts = [flat + (place_in + (STRIP * t - middle)) / middle * down for t in range(2)] + [across]
+            for p, part in enumerate(parts):
+                part_high, part_low = split(part)
+                stage[n % 2, p, 0, :, pl.ds(lo, LANE)] = part_high
+                stage[n % 2, p, 1, :, pl.ds(lo, LANE)] = part_low
+            return carry
+
+        lax.fori_loop(0, DEPTH // LANE, chunk, 0)
+        stores[n].start()
+
+    waiting = list(range(blocks))
+
+    def build_next():
+        if waiting:
+            build(waiting.pop(0))
+
     def moves_up(s):
         return jnp.logical_and(has_above, s <= tcol)
 
@@ -354,11 +400,14 @@
                 up_in = remote(slot(h, 0, s), slot(h, 0, s), z_up.at[h, s], z_recv.at[h, s], across_x)
                 up_in.wait_recv()
             column_item(h, s, j == 0)
+        build_next()
         if j > 0:
             for h in range(2):
                 partner_item(h, spots[j - 1])
+            build_next()
     for h in range(2):
         partner_item(h, spots[-1])
+    build_next()
     for w in range(2):
         for s in spots:
             for h in range(2):
@@ -367,6 +416,9 @@
                 )
                 two_in.wait_recv()
                 hand(h, 2 + w, s).start()
+            build_next()
+    while waiting:
+        build_next()
 
     other = lax.rem(trow, 2)
     for j, s in enumerate(spots):
@@ -376,6 +428,8 @@
                 landed = place(row + 1 - 2 * other, s, vis, h)
                 remote(landed, landed, k_send.at[h, w, s], k_recv.at[h, w, s], sibling).wait_recv()
     mine.wait()
+    for store in stores[-2:]:
+        store.wait()
     for j, s in enumerate(spots):
         fresh = j == 0
         for h in range(2):
@@ -394,24 +448,36 @@
                 hand(h, w, s, fresh and w == 0).wait_send()
 
 
-def gathered(template, columns, devices):
+def gathered(template, columns, devices, coeffs, spread_out, rows):
     order = [sorted(range(columns), key=lambda s: (abs(s - z), s)) for z in range(columns)]
     dma = pltpu.SemaphoreType.DMA
+    blocks = coeffs.shape[0]
+    listed = coeffs.transpose(0, 2, 1).reshape(blocks * 3, -1)
 
     def kernel(*refs):
         gather_kernel(columns, order, *refs)
 
     return pl.pallas_call(
         kernel,
-        in_specs=[pl.BlockSpec(memory_space=pl.ANY)],
-        out_specs=pl.BlockSpec(memory_space=pl.ANY),
-        out_shape=jax.ShapeDtypeStruct((devices * template.shape[0], template.shape[1]), template.dtype),
+        in_specs=[pl.BlockSpec(memory_space=pl.ANY)] * 4,
+        out_specs=[pl.BlockSpec(memory_space=pl.ANY)] * 2,
+        out_shape=[
+            jax.ShapeDtypeStruct((devices * template.shape[0], template.shape[1]), template.dtype),
+            jax.ShapeDtypeStruct((blocks, 3, 2, STRIP, DEPTH), jnp.bfloat16),
+        ],
         scratch_shapes=[
             dma((2, columns)), dma((2, columns)), dma((2, columns)),
             dma((2, columns)), dma((2, columns)),
             dma((2, 2, columns)), dma((2, 2, columns)),
             dma((2, 4, columns)), dma((2, 4, columns)),
             dma,
+            pltpu.VMEM(listed.shape, jnp.float32),
+            pltpu.VMEM(spread_out.shape, jnp.float32),
+            pltpu.VMEM(rows.shape, jnp.float32),
+            pltpu.VMEM((blocks * 3, spread_out.shape[1]), jnp.float32),
+            pltpu.VMEM((2, 3, 2, STRIP, DEPTH), jnp.bfloat16),
+            dma((3,)),
+            dma((2,)),
         ],
         compiler_params=pltpu.CompilerParams(
             collective_id=0, has_side_effects=True, vmem_limit_bytes=60 << 20
@@ -420,19 +486,24 @@
             flops=0, bytes_accessed=2 * devices * template.size * 4, transcendentals=0
         ),
         name="gather_template",
-    )(template)
+    )(template, listed, spread_out, rows)
 
 
 def on_device(template, warped, coeffs, dest_tile, position):
     axes = ("trow", "tcol", "visit")
     sizes = [lax.axis_size(axis) for axis in axes]
+    _, rows, spread_out = constants()
     if sizes[0] == 4 and sizes[2] == 2:
-        sky = gathered(template, sizes[1], sizes[0] * sizes[1] * sizes[2])
+        sky, mix = gathered(
+            template, sizes[1], sizes[0] * sizes[1] * sizes[2], coeffs, jnp.asarray(spread_out), jnp.asarray(rows)
+        )
     else:
         sky = lax.all_gather(template, axes, axis=0, tiled=True)
+        expanded = jnp.einsum("nbq,bk->nqk", coeffs, spread_out, precision=lax.Precision.HIGHEST)
+        mix = mixing(expanded, jnp.asarray(rows))
     subs = template.shape[1] // BLK
     return local_part(
-        sky, warped, coeffs, dest_tile[:, 0], position[:, 0],
+        sky, mix, warped, dest_tile[:, 0], position[:, 0],
         lax.axis_size("trow"), lax.axis_size("tcol"), subs,
     )
 

time: 143 us -> 124 us (0.87)
  Pallas kernels: 136 us -> 120 us
  matrix products: 2.75 us -> 0 us
    pallas_call x2 -> x1, Pallas kernels: 91.9 us -> 75.9 us  [gathered(): pl.pallas_call(kernel, in_specs=[pl.BlockSpec(memory_space=pl.ANY)] * 4,...]
    dot_general x1 -> x0, matrix products: 2.75 us -> none  [local_part(): jnp.einsum('nbq,bk->nqk', coeffs, spread_out, precision=lax.Precision.HIG...]
    reshape x0 -> x1, local copies, waits for them, and re-layouts: none -> 1.51 us  [gathered(): listed = coeffs.transpose(0, 2, 1).reshape(blocks * 3, -1)]
    unnamed x16 -> x10, local copies, waits for them, and re-layouts: 3.06 us -> 2.23 us
where the time goes in v1:
time: 124 us
  Pallas kernels  120 us (97%)
  local copies, waits for them, and re-layouts  3.73 us (3%)
    pallas_call x1, Pallas kernels, gathered(): pl.pallas_call(kernel, in_specs=[pl.BlockSpec(memory_space=pl.ANY)] * 4,...  75.9 us
    pallas_call x1, Pallas kernels, differences(): pl.pallas_call(kernel, grid_spec=pltpu.PrefetchScalarGridSpec(num_scalar_...  44.1 us

profile of v1, /device:TPU:1, one launch (start us, length us, event | category | flops | bytes accessed | tf_op | source)
XLA Modules:
  0.0 123.8 jit_solution(9342661516017061403)
XLA Ops:
  0.0 0.0 copy-start.2
  0.0 0.0 copy-start.1
  0.0 0.0 copy-start
  0.0 1.5 %reshape.3.refs_1_ = f32[36,27]{1,0:T(8,128)} reshape(f32[12,3,27]{2,1,0:T(4,128)} %bitcast.5) | data formatting | bytes 7776 | tf_op jit(solution)/shard_map/reshape | solution.py:455
  1.5 75.9 %gather_template.1 = (f32[8192,512]{1,0:T(8,128)}, bf16[12,3,2,128,1792]{4,3,2,1,0:T(8,128)(2,1)}) custom-call(f32[256,512]{1,0:T(8,128)} %refs_0_.1, f32[36,27]{1,0:T(8,128)} %reshape.3.refs_1_, f32[27,8960]{1,0:T(8,128)} %constant.8.clone.refs_2_, f32[5,128,1792]{2,1,0:T(8,128)} %constant.9.clone.refs_3_), custom_call_target="tpu_custom_call" | custom-call | bytes 33554432 | tf_op jit(solution)/shard_map/gather_template/pallas_call | solution.py:460
  77.4 0.0 copy-done.2
  77.4 0.0 copy-done.1
  77.5 0.0 copy-done
  77.5 0.0 copy-start.3
  77.5 1.1 copy-done.3
  78.6 0.0 copy-start.4
  78.6 1.1 copy-done.4
  79.7 44.1 %differences.1 = f32[12,256,256]{2,1,0:T(8,128)} custom-call(s32[12]{0:T(128)S(1)} %bitcast.3, s32[12]{0:T(128)S(1)} %bitcast.4, bf16[12,3,2,128,1792]{4,3,2,1,0:T(8,128)(2,1)} %get-tuple-element.7.refs_2_, f32[12,256,256]{2,1,0:T(8,128)S(1)} %copy-done, bf16[256,1408]{1,0:T(8,128)(2,1)S(1)} %copy-done.4, bf16[256,1408]{1,0:T(8,128)(2,1)S(1)} %copy-done.3, ...), custom_call_target="tpu_custom_call" | custom-call | flops 34800001024 | bytes 48000000 | tf_op jit(solution)/shard_map/differences/pallas_call | solution.py:205
Async XLA Ops:
  0.0 77.4 %copy-start.2 = (s32[12,1]{0,1:T(1,128)S(1)}, s32[12,1]{0,1:T(1,128)}, u32[]{:S(2)}) copy-start(s32[12,1]{0,1:T(1,128)} %param.13) | copy-start | bytes 148
  0.0 77.4 %copy-start.1 = (s32[12,1]{0,1:T(1,128)S(1)}, s32[12,1]{0,1:T(1,128)}, u32[]{:S(2)}) copy-start(s32[12,1]{0,1:T(1,128)} %param.12) | copy-start | bytes 148
  0.0 77.5 %copy-start = (f32[12,256,256]{2,1,0:T(8,128)S(1)}, f32[12,256,256]{2,1,0:T(8,128)}, u32[]{:S(2)}) copy-start(f32[12,256,256]{2,1,0:T(8,128)} %refs_3_.2) | copy-start | bytes 9437188
  77.5 1.1 copy-start.3
  78.6 1.1 copy-start.4
